TPU v7x, 512 devices: a whole 4x4x16 slice. The times are simulated.
512 devices in a mesh: tm: 16 (over z_lo, x), ctx: 32 (over y, z_hi, core).
Axes of the slice: x: 4, y: 4, z: 16 (z_hi: 4, z_lo: 4; z = z_hi * 4 + z_lo), core: 2. Of those that a mesh axis runs over, the one named last changes fastest.
Arguments:
- states: float32 [16, 3072, 64], P('tm', 'ctx'), may hold values from -6 to 6
- noise_draws: float32 [16, 3072, 64], P('tm', 'ctx'), may hold values from -6 to 6
- plan: int32 [17], replicated, may hold values from 0 to 1000, as said below
- w_embed: bfloat16 [64, 3072], replicated, may hold values from -0.75 to 0.75
- w_time: bfloat16 [128, 3072], replicated, may hold values from -0.5 to 0.5
- w_query: bfloat16 [16, 3072, 128], P('tm'), may hold values from -0.109375 to 0.109375
- w_key: bfloat16 [16, 3072, 128], P('tm'), may hold values from -0.109375 to 0.109375
- w_value: bfloat16 [16, 3072, 128], P('tm'), may hold values from -0.109375 to 0.109375
- gain_query: float32 [16, 128], P('tm'), may hold values from 0.5 to 16, as said below
- gain_key: float32 [16, 128], P('tm'), may hold values from 0.5 to 16, as said below
- w_out: bfloat16 [16, 128, 3072], P('tm'), may hold values from -0.5 to 0.5
- w_final: bfloat16 [3072, 64], replicated, may hold values from -0.109375 to 0.109375
Outputs:
- new_states: float32 [16, 3072, 64], P('tm', 'ctx')
Inputs may be any that keep to these rules, and one draw needn't show every extreme that they name: plan[0] is 1000 and each later entry is smaller than the one before by 31 to 61. `gain_query`: positive gains. `gain_key`: positive gains.
All inputs are finite; a program needn't handle non-finite values.
Results may differ from a plain program's by a relative error of at most 0.014.
The roundings to bfloat16 on the way count: a program that leaves them out, or rounds other values in their place, can miss the bound.
Values may be sent and summed in bfloat16 or wider, within the bound.
No kernel may reach another device: no remote copies, remote signals or barrier semaphores. Data moves between devices by JAX's collectives and lax.ppermute only.
A program may use at most 64 MiB of HBM per device.

v0:
```python
import math
import jax
import jax.numpy as jnp
from jax import lax
from jax.sharding import PartitionSpec as P


def with_halo(array, sides, width):
    for axis, dim in sides:
        size, length = (lax.axis_size(axis), array.shape[dim])
        up = [(i, (i + 1) % size) for i in range(size - 1)]
        down = [(j, i) for i, j in up]
        last = lax.slice_in_dim(array, length - width, length, axis=dim)
        first = lax.slice_in_dim(array, 0, width, axis=dim)
        before = lax.ppermute(last, axis, up)
        after = lax.ppermute(first, axis, down)
        array = jnp.concatenate([before, array, after], axis=dim)
    return array


def entering(value, axis, join, neutral):
    count, mine = (lax.axis_size(axis), lax.axis_index(axis))
    pieces = lax.all_gather(value, axis)
    total = jnp.full_like(value, 0) + jnp.asarray(neutral, value.dtype)

    def hop(position, total):
        longer = join(total, pieces[position])
        return jnp.where(position < mine, longer, total)

    return lax.fori_loop(0, count - 1, hop, total)


def fourier_rows(plan, freq_count, step_count):
    half_freq = freq_count // 2
    frequency = jnp.exp(-math.log(10000.0) * jnp.arange(half_freq, dtype=jnp.float32) / half_freq)
    phase_arg = plan[:step_count].astype(jnp.float32)[:, None] * frequency[None, :]
    return jnp.concatenate([jnp.cos(phase_arg), jnp.sin(phase_arg)], axis=1).astype(jnp.bfloat16)


def rms_gain(values_in, gain_row):
    scale = lax.rsqrt(jnp.mean(values_in * values_in, axis=-1, keepdims=True) + 1e-06)
    return values_in * scale * gain_row


def per_device(
    states,
    noise_draws,
    plan,
    w_embed,
    w_time,
    w_query,
    w_key,
    w_value,
    gain_query,
    gain_key,
    w_out,
    w_final,
):
    every = lax.all_gather(states, "tm", axis=0, tiled=True)
    nsteps, tok_rows, channels = every.shape
    own_steps = states.shape[0]
    model_width = w_embed.shape[1]
    head_dim = w_query.shape[2]
    ctx_count = lax.axis_size("ctx")
    ctx_index = lax.axis_index("ctx")
    tm_index = lax.axis_index("tm")
    features = fourier_rows(plan, w_time.shape[0], nsteps)
    time_shift = jnp.dot(features, w_time, preferred_element_type=jnp.float32)
    latents = every.astype(jnp.bfloat16)
    count = latents.shape[1]
    embedded = jnp.dot(
        latents.reshape(nsteps * count, channels), w_embed, preferred_element_type=jnp.float32
    )
    hidden = (embedded.reshape(nsteps, count, model_width) + time_shift[:, None, :]).astype(
        jnp.bfloat16
    )
    count = hidden.shape[1]
    flat_rows = hidden.reshape(nsteps * count, model_width)
    key_rows = rms_gain(
        jnp.dot(flat_rows, w_key[0], preferred_element_type=jnp.float32), gain_key[0]
    ).astype(jnp.bfloat16)
    value_rows = jnp.dot(flat_rows, w_value[0], preferred_element_type=jnp.float32).astype(
        jnp.bfloat16
    )
    key_value = with_halo(
        jnp.concatenate([key_rows, value_rows], axis=1).reshape(nsteps, count, 2 * head_dim),
        (("ctx", 1),),
        tok_rows,
    )
    flat_hidden = hidden.reshape(nsteps * tok_rows, model_width)
    queries = rms_gain(
        jnp.dot(flat_hidden, w_query[0], preferred_element_type=jnp.float32), gain_query[0]
    ).astype(jnp.bfloat16)
    queries = queries.reshape(nsteps, tok_rows, head_dim)
    key_part = key_value[..., :head_dim]
    value_part = key_value[..., head_dim:]
    block_of = jnp.arange(3 * tok_rows, dtype=jnp.int32) // tok_rows
    valid = (
        (block_of == 1)
        | (block_of == 0) & (ctx_index > 0)
        | (block_of == 2) & (ctx_index < ctx_count - 1)
    )
    valid = valid[None, None, :]
    scores = jnp.einsum(
        "sqe,ske->sqk", queries, key_part, preferred_element_type=jnp.float32
    ) / math.sqrt(head_dim)
    top_score = jnp.max(jnp.where(valid, scores, -1e30), axis=-1, keepdims=True)
    expo = jnp.where(valid, jnp.exp(scores - top_score), 0.0)
    attn_probs = (expo / jnp.sum(expo, axis=-1, keepdims=True)).astype(jnp.bfloat16)
    attended = jnp.einsum(
        "sqk,ske->sqe", attn_probs, value_part, preferred_element_type=jnp.float32
    ).astype(jnp.bfloat16)
    projected = jnp.dot(
        attended.reshape(nsteps * tok_rows, head_dim), w_out[0], preferred_element_type=jnp.float32
    ).astype(jnp.bfloat16)
    head_terms = jnp.dot(projected, w_final, preferred_element_type=jnp.float32).reshape(
        nsteps, tok_rows, channels
    )
    own_hidden = lax.dynamic_slice_in_dim(hidden, tm_index * own_steps, own_steps, 0)
    residual = jnp.dot(
        own_hidden.reshape(own_steps * tok_rows, model_width),
        w_final,
        preferred_element_type=jnp.float32,
    )
    residual = residual.reshape(own_steps, tok_rows, channels)
    step_sizes = (plan[:-1] - plan[1:]).astype(jnp.float32) / 1000.0
    own_sizes = lax.dynamic_slice_in_dim(step_sizes, tm_index * own_steps, own_steps, 0)
    start_state = every[0][None, :, :]
    drift_rows = lax.psum_scatter(head_terms, "tm", scatter_dimension=0, tiled=True) + residual
    increment = (
        own_sizes[:, None, None] * drift_rows + jnp.sqrt(own_sizes)[:, None, None] * noise_draws
    )
    running = jnp.cumsum(increment, axis=0)
    earlier = entering(running[-1], "tm", jnp.add, jnp.zeros_like(running[-1]))
    return start_state + earlier[None, :, :] + running


def solution(mesh):
    return jax.shard_map(
        per_device,
        mesh=mesh,
        in_specs=(
            P("tm", "ctx", None),
            P("tm", "ctx", None),
            P(),
            P(),
            P(),
            P("tm", None, None),
            P("tm", None, None),
            P("tm", None, None),
            P("tm", None),
            P("tm", None),
            P("tm", None, None),
            P(),
        ),
        out_specs=P("tm", "ctx", None),
        check_vma=False,
    )
```

profile of v0, /device:TPU:8, one launch (start us, length us, event | category | flops | bytes accessed | tf_op | source)
XLA Modules:
  0.0 257.8 jit_solution(12405270481454556288)
XLA Ops:
  6.5 0.7 slice_convert_fusion
  7.3 46.7 %all_gather.6 = f32[16,96,64]{1,2,0:T(8,128)S(1)} all-gather(f32[1,96,64]{1,2,0:T(8,128)} %param.14), channel_id=1, replica_groups=mesh['tm'=16,'ctx'=32] {'tm'}, dimensions={0}, use_global_device_ids=true | all-gather | bytes 417792 | tf_op jit(solution)/shard_map/all_gather | solution.py:59
  54.0 0.1 fusion.27
  54.1 1.4 fusion.29
  55.5 3.9 %add_convert_fusion = bf16[16,96,3072]{2,1,0:T(8,128)(2,1)S(1)} fusion(f32[16,3072]{1,0:T(8,128)S(1)} %fusion.29, bf16[64,3072]{1,0:T(8,128)(2,1)} %param.17, f32[16,96,64]{1,2,0:T(8,128)S(1)} %all_gather.6), kind=kOutput, calls=%fused_computation.3 | convolution fusion | flops 613515264 | bytes 10420224 | tf_op jit(solution)/shard_map/dot_general | solution.py:71
  59.4 3.3 %multiply_reduce_fusion = (f32[1536]{0:T(1024)S(1)}, f32[1536,128]{0,1:T(8,128)S(1)}) fusion(bf16[1536,3072]{1,0:T(8,128)(2,1)S(1)} %bitcast.55, bf16[1,3072,128]{2,1,0:T(8,128)(2,1)S(1)} %copy-done), kind=kOutput, calls=%fused_computation.32 | convolution fusion | flops 1208351232 | bytes 11016192 | tf_op jit(solution)/shard_map/dot_general | solution.py:80
  62.7 0.3 copy-done.1
  63.0 3.3 %convolution_convert_fusion.1 = bf16[1536,128]{0,1:T(8,128)(2,1)S(1)} fusion(bf16[1536,3072]{1,0:T(8,128)(2,1)S(1)} %bitcast.56, bf16[1,3072,128]{2,1,0:T(8,128)(2,1)S(1)} %copy-done.2), kind=kOutput, calls=%fused_computation.6 | convolution fusion | flops 1208156160 | bytes 10616832 | tf_op jit(solution)/shard_map/dot_general | solution.py:82
  66.3 0.1 multiply_convert_fusion
  66.5 0.3 copy.22
  66.7 1.9 collective-permute-start
  68.7 8.6 %collective-permute-start.1 = (bf16[16,96,256]{2,1,0:T(8,128)(2,1)S(1)}, bf16[16,96,256]{2,1,0:T(8,128)(2,1)}, u32[]{:S(2)}, u32[]{:S(2)}) collective-permute-start(bf16[16,96,256]{2,1,0:T(8,128)(2,1)S(1)} %bitcast.59), channel_id=1, source_target_pairs={{1,0},{2,1},{3,2},{4,3},{5,4},{6,5},{7,6},{8,7},{9,8},{10,9},{11,1... | collective-permute-start | bytes 2359304 | tf_op jit(solution)/shard_map/ppermute | solution.py:16
  77.3 5.5 %multiply_reduce_fusion.1 = (f32[1536]{0:T(1024)S(1)}, f32[1536,128]{1,0:T(8,128)S(1)}) fusion(bf16[1536,3072]{1,0:T(8,128)(2,1)} %bitcast.57, bf16[1,3072,128]{2,1,0:T(8,128)(2,1)} %param.19), kind=kOutput, calls=%fused_computation.34 | convolution fusion | flops 1208351232 | bytes 11016192 | tf_op jit(solution)/shard_map/dot_general | solution.py:92
  82.9 0.3 multiply_convert_fusion.1
  83.2 24.8 %collective-permute-done = bf16[16,96,256]{2,1,0:T(8,128)(2,1)} collective-permute-done((bf16[16,96,256]{2,1,0:T(8,128)(2,1)S(1)}, bf16[16,96,256]{2,1,0:T(8,128)(2,1)}, u32[]{:S(2)}, u32[]{:S(2)}) %collective-permute-start) | collective-permute-done | bytes 786464 | tf_op jit(solution)/shard_map/ppermute | solution.py:15
  107.9 1.5 pad_maximum_fusion
  109.5 0.7 fusion.7
  110.2 1.0 fusion.40
  111.2 0.6 convolution_convert_fusion.2
  111.8 0.3 copy-done.3
  112.1 0.3 copy-done.7
  112.4 5.4 %fusion.1 = f32[1536,64]{0,1:T(8,128)S(1)} fusion(bf16[3072,64]{0,1:T(8,128)(2,1)S(1)} %copy-done.3, bf16[1536,128]{1,0:T(8,128)(2,1)S(1)} %bitcast.64, bf16[1,128,3072]{2,1,0:T(8,128)(2,1)S(1)} %copy-done.7), kind=kOutput, calls=%fused_computation.5 | convolution fusion | flops 1816657920 | bytes 1966080 | tf_op jit(solution)/shard_map/dot_general | solution.py:116
  117.8 0.2 reshape.81
  118.0 0.9 copy.23
  119.0 0.6 dynamic_slice.13
  120.2 85.3 %reduce-scatter.2.cloned.1.call-done = f32[1,96,64]{1,2,0:T(8,128)} async-done(((f32[16,96,64]{1,2,0:T(8,128)}), f32[1,96,64]{1,2,0:T(8,128)}) %reduce-scatter.2.cloned.1.call-update) | async-done | bytes 24592 | tf_op jit(solution)/shard_map/reduce_scatter | solution.py:129
  205.5 1.9 fusion.14
  207.5 40.5 %all_gather.7 = f32[16,96,64]{1,2,0:T(8,128)S(1)} all-gather(f32[1,96,64]{1,2,0:T(8,128)S(1)} %fusion.14), channel_id=1, replica_groups=mesh['tm'=16,'ctx'=32] {'tm'}, dimensions={0}, use_global_device_ids=true | all-gather | bytes 417792 | tf_op jit(solution)/shard_map/all_gather | solution.py:23
  248.0 2.2 while.14
  248.0 0.1 copy.28
  248.3 0.1 copy.28
  250.3 0.6 fusion.26
  (69 shorter events, 1.7 us)
Async XLA Ops:
  6.5 52.9 %copy-start = (bf16[1,3072,128]{2,1,0:T(8,128)(2,1)S(1)}, bf16[1,3072,128]{2,1,0:T(8,128)(2,1)}, u32[]{:S(2)}) copy-start(bf16[1,3072,128]{2,1,0:T(8,128)(2,1)} %param.20) | copy-start | bytes 2359300
  6.5 199.0 %reduce-scatter.2.cloned.1.call-start = ((), (), s32[]{:S(2)}) async-start(), calls=%async_computation.1 | async-start | bytes 557056 | tf_op jit(solution)/shard_map/reduce_scatter | solution.py:129
  59.4 3.6 %copy-start.1 = (bf16[16,96,3072]{2,1,0:T(8,128)(2,1)}, bf16[16,96,3072]{2,1,0:T(8,128)(2,1)S(1)}, u32[]{:S(2)}) copy-start(bf16[16,96,3072]{2,1,0:T(8,128)(2,1)S(1)} %add_convert_fusion) | copy-start | bytes 28311556
  59.4 3.6 %copy-start.2 = (bf16[1,3072,128]{2,1,0:T(8,128)(2,1)S(1)}, bf16[1,3072,128]{2,1,0:T(8,128)(2,1)}, u32[]{:S(2)}) copy-start(bf16[1,3072,128]{2,1,0:T(8,128)(2,1)} %param.21) | copy-start | bytes 2359300
  63.0 3.3 %copy-start.5 = (f32[1,128]{1,0:T(1,128)S(1)}, f32[1,128]{1,0:T(1,128)}, u32[]{:S(2)}) copy-start(f32[1,128]{1,0:T(1,128)} %param.23) | copy-start | bytes 1540
  66.7 41.2 %collective-permute-start = (bf16[16,96,256]{2,1,0:T(8,128)(2,1)S(1)}, bf16[16,96,256]{2,1,0:T(8,128)(2,1)}, u32[]{:S(2)}, u32[]{:S(2)}) collective-permute-start(bf16[16,96,256]{2,1,0:T(8,128)(2,1)S(1)} %bitcast.58), channel_id=1, source_target_pairs={{0,1},{1,2},{2,3},{3,4},{4,5},{5,6},{6,7},{7,8},{8,9},{9,10},{10,1... | collective-permute-start | bytes 2359304 | tf_op jit(solution)/shard_map/ppermute | solution.py:15
  68.7 39.3 %collective-permute-start.1 = (bf16[16,96,256]{2,1,0:T(8,128)(2,1)S(1)}, bf16[16,96,256]{2,1,0:T(8,128)(2,1)}, u32[]{:S(2)}, u32[]{:S(2)}) collective-permute-start(bf16[16,96,256]{2,1,0:T(8,128)(2,1)S(1)} %bitcast.59), channel_id=1, source_target_pairs={{1,0},{2,1},{3,2},{4,3},{5,4},{6,5},{7,6},{8,7},{9,8},{10,9},{11,1... | collective-permute-start | bytes 2359304 | tf_op jit(solution)/shard_map/ppermute | solution.py:16
  77.3 5.5 %copy-start.6 = (f32[1,128]{1,0:T(1,128)S(1)}, f32[1,128]{1,0:T(1,128)}, u32[]{:S(2)}) copy-start(f32[1,128]{1,0:T(1,128)} %param.22) | copy-start | bytes 1540
  111.1 1.0 copy-start.3
  111.2 1.2 copy-start.7
  117.8 1.2 copy-start.8
  117.8 87.8 %copy-start.4 = (f32[1,96,64]{1,2,0:T(8,128)S(1)}, f32[1,96,64]{1,2,0:T(8,128)}, u32[]{:S(2)}) copy-start(f32[1,96,64]{1,2,0:T(8,128)} %param.15) | copy-start | bytes 73732
Sparse Core Ops, SparseCore 0:
  119.1 86.4 reduce-scatter.1
where the time goes:
time: 258 us
  waiting for transfers between devices  110 us (43%)
  blocking collectives  87.3 us (34%)
  matrix products  25.9 us (10%)
  between operations  14.2 us (6%)
  starting transfers between devices  10.6 us (4%)
  other arithmetic  4.76 us (2%)
  local copies, waits for them, and re-layouts  4.32 us (2%)
    reduce_scatter x1, waiting for transfers between devices, per_device(): lax.psum_scatter(head_terms, 'tm', scatter_dimension=0, tiled=True)  85.3 us
    all_gather x1, blocking collectives, per_device(): every = lax.all_gather(states, 'tm', axis=0, tiled=True)  46.7 us
    all_gather x1, blocking collectives, entering(): pieces = lax.all_gather(value, axis)  40.5 us
    ppermute x1, waiting for transfers between devices, with_halo(): before = lax.ppermute(last, axis, up)  24.8 us
    ppermute x1, starting transfers between devices, with_halo(): after = lax.ppermute(first, axis, down)  8.63 us
    dot_general x1, matrix products, per_device(): jnp.dot(flat_hidden, w_query[0], preferred_element_type=jnp.float32)  5.49 us
    dot_general x1, matrix products, per_device(): jnp.dot(projected, w_final, preferred_element_type=jnp.float32)  5.35 us
  transfers between devices with their start and end apart: 3, of which 2 were waited for; matrix products, arithmetic and copies ran while one was open for 2% of the time, Pallas kernels for 0%

commit v1 on v0

--- a/solution.py
+++ b/solution.py
@@ -56,7 +56,8 @@
     w_out,
     w_final,
 ):
-    every = lax.all_gather(states, "tm", axis=0, tiled=True)
+    repeated = jnp.stack([states] * lax.axis_size("tm"))
+    every = jnp.concatenate(lax.all_to_all(repeated, "tm", 0, 0), axis=0)
     nsteps, tok_rows, channels = every.shape
     own_steps = states.shape[0]
     model_width = w_embed.shape[1]

time: 258 us -> 241 us (0.934)
  the two profiles are of different devices: /device:TPU:8 before, /device:TPU:16 now
where the time goes in v1:
time: 241 us; the launch traced here: 240 us
  waiting for transfers between devices  131 us (54%)
  blocking collectives  40.5 us (17%)
  matrix products  24.9 us (10%)
  starting transfers between devices  19.1 us (8%)
  between operations  14.3 us (6%)
  local copies, waits for them, and re-layouts  6.09 us (3%)
  other arithmetic  3.32 us (1%)
    reduce_scatter x1, waiting for transfers between devices, per_device(): lax.psum_scatter(head_terms, 'tm', scatter_dimension=0, tiled=True)  89.5 us
    all_gather x1, blocking collectives, entering(): pieces = lax.all_gather(value, axis)  40.5 us
    ppermute x1, waiting for transfers between devices, with_halo(): after = lax.ppermute(first, axis, down)  22.3 us
    all_to_all x1, waiting for transfers between devices, per_device(): every = jnp.concatenate(lax.all_to_all(repeated, 'tm', 0, 0), axis=0)  13.2 us
    ppermute x1, starting transfers between devices, with_halo(): after = lax.ppermute(first, axis, down)  8.63 us
    all_to_all x1, starting transfers between devices, per_device(): every = jnp.concatenate(lax.all_to_all(repeated, 'tm', 0, 0), axis=0)  8.47 us
    ppermute x1, waiting for transfers between devices, with_halo(): before = lax.ppermute(last, axis, up)  6.55 us
    dot_general x1, matrix products, per_device(): jnp.dot(flat_hidden, w_query[0], preferred_element_type=jnp.float32)  5.48 us
  transfers between devices with their start and end apart: 4, of which 4 were waited for; matrix products, arithmetic and copies ran while one was open for 4% of the time, Pallas kernels for 0%

profile of v1, /device:TPU:16, one launch (start us, length us, event | category | flops | bytes accessed | tf_op | source)
XLA Modules:
  0.0 240.3 jit_solution(3448954836697229609)
XLA Ops:
  6.5 1.7 stack.2
  8.2 8.5 %all-to-all-start = ((f32[16,1,96,64]{2,3,1,0:T(8,128)}), f32[16,1,96,64]{2,3,1,0:T(8,128)S(1)}, u32[]{:S(2)}, u32[]{:S(2)}) async-start(f32[16,1,96,64]{2,3,1,0:T(8,128)} %stack.2), calls=%async_computation | async-start | bytes 1048576 | tf_op jit(solution)/shard_map/all_to_all | solution.py:60
  16.8 0.7 slice_convert_fusion
  17.6 1.4 fusion.32
  19.0 13.2 %all-to-all-done = f32[16,1,96,64]{2,3,1,0:T(8,128)S(1)} async-done(((f32[16,1,96,64]{2,3,1,0:T(8,128)}), f32[16,1,96,64]{2,3,1,0:T(8,128)S(1)}, u32[]{:S(2)}, u32[]{:S(2)}) %all-to-all-start) | async-done | bytes 393248 | tf_op jit(solution)/shard_map/all_to_all | solution.py:60
  32.2 2.8 %add_convert_fusion = bf16[16,96,3072]{2,1,0:T(8,128)(2,1)S(1)} fusion(f32[16,3072]{1,0:T(8,128)S(1)} %fusion.32, bf16[64,3072]{1,0:T(8,128)(2,1)S(1)} %copy-done.3, f32[16,1,96,64]{2,3,1,0:T(8,128)S(1)} %all-to-all-done), kind=kOutput, calls=%fused_computation.3 | convolution fusion | flops 613515264 | bytes 10420224 | tf_op jit(solution)/shard_map/dot_general | solution.py:72
  35.0 3.3 %multiply_reduce_fusion = (f32[1536]{0:T(1024)S(1)}, f32[1536,128]{0,1:T(8,128)S(1)}) fusion(bf16[1536,3072]{1,0:T(8,128)(2,1)S(1)} %bitcast.74, bf16[1,3072,128]{2,1,0:T(8,128)(2,1)S(1)} %copy-done), kind=kOutput, calls=%fused_computation.32 | convolution fusion | flops 1208351232 | bytes 11016192 | tf_op jit(solution)/shard_map/dot_general | solution.py:81
  38.3 0.3 copy-done.1
  38.6 3.3 %convolution_convert_fusion.1 = bf16[1536,128]{0,1:T(8,128)(2,1)S(1)} fusion(bf16[1536,3072]{1,0:T(8,128)(2,1)S(1)} %bitcast.75, bf16[1,3072,128]{2,1,0:T(8,128)(2,1)S(1)} %copy-done.2), kind=kOutput, calls=%fused_computation.6 | convolution fusion | flops 1208156160 | bytes 10616832 | tf_op jit(solution)/shard_map/dot_general | solution.py:83
  41.9 0.1 multiply_convert_fusion
  42.1 0.3 copy.23
  42.4 1.9 collective-permute-start
  44.3 8.6 %collective-permute-start.1 = (bf16[16,96,256]{2,1,0:T(8,128)(2,1)S(1)}, bf16[16,96,256]{2,1,0:T(8,128)(2,1)S(1)}, u32[]{:S(2)}, u32[]{:S(2)}) collective-permute-start(bf16[16,96,256]{2,1,0:T(8,128)(2,1)S(1)} %bitcast.78), channel_id=1, source_target_pairs={{1,0},{2,1},{3,2},{4,3},{5,4},{6,5},{7,6},{8,7},{9,8},{10,9},{11,1... | collective-permute-start | bytes 2359304 | tf_op jit(solution)/shard_map/ppermute | solution.py:16
  53.0 5.5 %multiply_reduce_fusion.1 = (f32[1536]{0:T(1024)S(1)}, f32[1536,128]{1,0:T(8,128)S(1)}) fusion(bf16[1536,3072]{1,0:T(8,128)(2,1)} %bitcast.76, bf16[1,3072,128]{2,1,0:T(8,128)(2,1)} %param.19), kind=kOutput, calls=%fused_computation.34 | convolution fusion | flops 1208351232 | bytes 11016192 | tf_op jit(solution)/shard_map/dot_general | solution.py:93
  58.5 0.3 multiply_convert_fusion.1
  58.7 6.5 %collective-permute-done = bf16[16,96,256]{2,1,0:T(8,128)(2,1)S(1)} collective-permute-done((bf16[16,96,256]{2,1,0:T(8,128)(2,1)S(1)}, bf16[16,96,256]{2,1,0:T(8,128)(2,1)S(1)}, u32[]{:S(2)}, u32[]{:S(2)}) %collective-permute-start) | collective-permute-done | bytes 786464 | tf_op jit(solution)/shard_map/ppermute | solution.py:15
  65.3 22.3 %collective-permute-done.1 = bf16[16,96,256]{2,1,0:T(8,128)(2,1)S(1)} collective-permute-done((bf16[16,96,256]{2,1,0:T(8,128)(2,1)S(1)}, bf16[16,96,256]{2,1,0:T(8,128)(2,1)S(1)}, u32[]{:S(2)}, u32[]{:S(2)}) %collective-permute-start.1) | collective-permute-done | bytes 786464 | tf_op jit(solution)/shard_map/ppermute | solution.py:16
  87.6 0.2 pad_maximum_fusion
  87.7 0.7 fusion.7
  88.4 1.0 fusion.43
  89.4 0.6 convolution_convert_fusion.2
  90.1 0.4 copy-done.4
  90.4 0.3 copy-done.8
  90.7 5.4 %fusion.1 = f32[1536,64]{0,1:T(8,128)S(1)} fusion(bf16[3072,64]{0,1:T(8,128)(2,1)S(1)} %copy-done.4, bf16[1536,128]{1,0:T(8,128)(2,1)S(1)} %bitcast.84, bf16[1,128,3072]{2,1,0:T(8,128)(2,1)S(1)} %copy-done.8), kind=kOutput, calls=%fused_computation.5 | convolution fusion | flops 1816657920 | bytes 1966080 | tf_op jit(solution)/shard_map/dot_general | solution.py:117
  96.0 0.2 reshape.90
  96.2 1.0 copy.24
  97.3 0.6 dynamic_slice.13
  98.6 89.5 %reduce-scatter.2.cloned.1.call-done = f32[1,96,64]{1,2,0:T(8,128)} async-done(((f32[16,96,64]{1,2,0:T(8,128)}), f32[1,96,64]{1,2,0:T(8,128)}) %reduce-scatter.2.cloned.1.call-update) | async-done | bytes 24592 | tf_op jit(solution)/shard_map/reduce_scatter | solution.py:130
  188.0 2.0 fusion.14
  190.0 40.5 %all_gather.3 = f32[16,96,64]{1,2,0:T(8,128)S(1)} all-gather(f32[1,96,64]{1,2,0:T(8,128)S(1)} %fusion.14), channel_id=1, replica_groups=mesh['tm'=16,'ctx'=32] {'tm'}, dimensions={0}, use_global_device_ids=true | all-gather | bytes 417792 | tf_op jit(solution)/shard_map/all_gather | solution.py:23
  230.5 2.2 while.14
  232.8 0.6 fusion.29
  (73 shorter events, 2.1 us)
Async XLA Ops:
  6.5 28.5 %copy-start = (bf16[1,3072,128]{2,1,0:T(8,128)(2,1)S(1)}, bf16[1,3072,128]{2,1,0:T(8,128)(2,1)}, u32[]{:S(2)}) copy-start(bf16[1,3072,128]{2,1,0:T(8,128)(2,1)} %param.20) | copy-start | bytes 2359300
  6.5 25.6 %copy-start.3 = (bf16[64,3072]{1,0:T(8,128)(2,1)S(1)}, bf16[64,3072]{1,0:T(8,128)(2,1)}, u32[]{:S(2)}) copy-start(bf16[64,3072]{1,0:T(8,128)(2,1)} %param.17) | copy-start | bytes 1179652
  8.2 23.9 %all-to-all-start = ((f32[16,1,96,64]{2,3,1,0:T(8,128)}), f32[16,1,96,64]{2,3,1,0:T(8,128)S(1)}, u32[]{:S(2)}, u32[]{:S(2)}) async-start(f32[16,1,96,64]{2,3,1,0:T(8,128)} %stack.2), calls=%async_computation | async-start | bytes 1048576 | tf_op jit(solution)/shard_map/all_to_all | solution.py:60
  16.7 171.3 %reduce-scatter.2.cloned.1.call-start = ((), (), s32[]{:S(2)}) async-start(), calls=%async_computation.2 | async-start | bytes 557056 | tf_op jit(solution)/shard_map/reduce_scatter | solution.py:130
  35.0 3.6 %copy-start.1 = (bf16[16,96,3072]{2,1,0:T(8,128)(2,1)}, bf16[16,96,3072]{2,1,0:T(8,128)(2,1)S(1)}, u32[]{:S(2)}) copy-start(bf16[16,96,3072]{2,1,0:T(8,128)(2,1)S(1)} %add_convert_fusion) | copy-start | bytes 28311556
  35.0 3.6 %copy-start.2 = (bf16[1,3072,128]{2,1,0:T(8,128)(2,1)S(1)}, bf16[1,3072,128]{2,1,0:T(8,128)(2,1)}, u32[]{:S(2)}) copy-start(bf16[1,3072,128]{2,1,0:T(8,128)(2,1)} %param.21) | copy-start | bytes 2359300
  38.6 3.3 %copy-start.6 = (f32[1,128]{1,0:T(1,128)S(1)}, f32[1,128]{1,0:T(1,128)}, u32[]{:S(2)}) copy-start(f32[1,128]{1,0:T(1,128)} %param.23) | copy-start | bytes 1540
  42.4 16.1 %copy-start.7 = (f32[1,128]{1,0:T(1,128)S(1)}, f32[1,128]{1,0:T(1,128)}, u32[]{:S(2)}) copy-start(f32[1,128]{1,0:T(1,128)} %param.22) | copy-start | bytes 1540
  42.4 22.9 %collective-permute-start = (bf16[16,96,256]{2,1,0:T(8,128)(2,1)S(1)}, bf16[16,96,256]{2,1,0:T(8,128)(2,1)S(1)}, u32[]{:S(2)}, u32[]{:S(2)}) collective-permute-start(bf16[16,96,256]{2,1,0:T(8,128)(2,1)S(1)} %bitcast.77), channel_id=1, source_target_pairs={{0,1},{1,2},{2,3},{3,4},{4,5},{5,6},{6,7},{7,8},{8,9},{9,10},{10,1... | collective-permute-start | bytes 2359304 | tf_op jit(solution)/shard_map/ppermute | solution.py:15
  44.3 43.3 %collective-permute-start.1 = (bf16[16,96,256]{2,1,0:T(8,128)(2,1)S(1)}, bf16[16,96,256]{2,1,0:T(8,128)(2,1)S(1)}, u32[]{:S(2)}, u32[]{:S(2)}) collective-permute-start(bf16[16,96,256]{2,1,0:T(8,128)(2,1)S(1)} %bitcast.78), channel_id=1, source_target_pairs={{1,0},{2,1},{3,2},{4,3},{5,4},{6,5},{7,6},{8,7},{9,8},{10,9},{11,1... | collective-permute-start | bytes 2359304 | tf_op jit(solution)/shard_map/ppermute | solution.py:16
  89.4 1.0 copy-start.4
  89.4 1.2 copy-start.8
  96.0 1.2 copy-start.9
  96.0 92.0 %copy-start.5 = (f32[1,96,64]{1,2,0:T(8,128)S(1)}, f32[1,96,64]{1,2,0:T(8,128)}, u32[]{:S(2)}) copy-start(f32[1,96,64]{1,2,0:T(8,128)} %param.15) | copy-start | bytes 73732
Sparse Core Ops, SparseCore 0:
  97.3 90.6 reduce-scatter.1
